TPU v7x, 128 devices: a whole 4x4x4 slice. The times are simulated.
128 devices in a mesh: grp: 2 (over core), tx: 8 (over x_lo, z), ty: 8 (over x_hi, y).
Axes of the slice: x: 4 (x_hi: 2, x_lo: 2; x = x_hi * 2 + x_lo), y: 4, z: 4, core: 2. Of those that a mesh axis runs over, the one named last changes fastest.
Arguments:
- expert_hidden: bfloat16 [2, 64, 8192], P(None, None, 'ty'), may hold values from -400 to 400
- expert_gain: bfloat16 [8192], P('ty'), may hold values from 0.5 to 1.5
- expert_query: bfloat16 [8192, 8192], P('ty', 'tx'), may hold values from -0.0625 to 0.0625
- expert_keys: bfloat16 [8192, 1024], P('ty', 'tx'), may hold values from -0.25 to 0.25
- expert_values: bfloat16 [8192, 1024], P('ty', 'tx'), may hold values from -0.0625 to 0.0625
- expert_output: bfloat16 [8192, 8192], P('tx', 'ty'), may hold values from -0.25 to 0.25
- expert_final: bfloat16 [8192], P('ty'), may hold values from 0.5 to 1.5
- expert_head: bfloat16 [32000, 8192], P(('grp', 'tx'), 'ty'), may hold values from -400 to 400
- expert_keycache: bfloat16 [64, 1024, 1024], P(('grp', 'ty'), None, 'tx'), may hold values from -400 to 400
- expert_valcache: bfloat16 [64, 1024, 1024], P(('grp', 'ty'), None, 'tx'), may hold values from -6 to 6
- amateur_hidden: bfloat16 [2, 64, 4096], P(None, None, 'ty'), may hold values from -400 to 400
- amateur_gain: bfloat16 [4096], P('ty'), may hold values from 0.5 to 1.5
- amateur_query: bfloat16 [4096, 4096], P('ty', 'tx'), may hold values from -0.09375 to 0.09375
- amateur_keys: bfloat16 [4096, 4096], P('ty', 'tx'), may hold values from -0.375 to 0.375
- amateur_values: bfloat16 [4096, 4096], P('ty', 'tx'), may hold values from -0.09375 to 0.09375
- amateur_output: bfloat16 [4096, 4096], P('tx', 'ty'), may hold values from -0.375 to 0.375
- amateur_final: bfloat16 [4096], P('ty'), may hold values from 0.5 to 1.5
- amateur_head: bfloat16 [32000, 4096], P(('grp', 'tx'), 'ty'), may hold values from -400 to 400
- amateur_keycache: bfloat16 [64, 1024, 4096], P(('grp', 'ty'), None, 'tx'), may hold values from -400 to 400
- amateur_valcache: bfloat16 [64, 1024, 4096], P(('grp', 'ty'), None, 'tx'), may hold values from -6 to 6
- lengths: int32 [64], P(('grp', 'ty')), may hold values from 1 to 1022, as said below
- tokens: int32 [2, 64], P(None, 'ty'), may hold values from 0 to 31999
Outputs:
- contrast: float32 [2, 64, 32000], P(None, 'ty', ('grp', 'tx'))
- token_score: float32 [2, 64], P(None, 'ty')
Inputs may be any that keep to these rules, and one draw needn't show every extreme that they name: Row r's prompt fills cache positions 0 to lengths[r] - 1; the later cache positions hold no data.
All inputs are finite; a program needn't handle non-finite values.
Results may differ from a plain program's by a relative error of at most 0.012.
The roundings to bfloat16 on the way count: a program that leaves them out, or rounds other values in their place, can miss the bound.
Values may be sent and summed in bfloat16 or wider, within the bound.
A program may use at most 128 MiB of HBM per device.

v0:
```python
import functools
import math

import jax
import jax.numpy as jnp
from jax import lax
from jax.experimental import pallas as pl
from jax.experimental.pallas import tpu as pltpu
from jax.sharding import PartitionSpec as P

HEAD = 128
EPS = 1e-05
BASE = 10000.0
AMATEUR = 0.5
SCALE = HEAD**-0.5
CHUNK = 512
SLAB = 1024
F32 = jnp.float32
BF16 = jnp.bfloat16
MESH = pl.DeviceIdType.MESH


def iota(shape, axis):
    return lax.broadcasted_iota(jnp.int32, shape, axis)


def mm(a, b):
    return lax.dot_general(a, b, (((1,), (0,)), ((), ())), preferred_element_type=F32)


def mm_t(a, b):
    return lax.dot_general(a, b, (((1,), (1,)), ((), ())), preferred_element_type=F32)


def one_hot(size, source):
    out = iota((size, size), 0)
    return jnp.where(iota((size, size), 1) == source(out), 1.0, 0.0).astype(BF16)


def folded(values):
    half = values.shape[-1] // 2
    return jnp.concatenate([values[..., :half], values[..., half:]], axis=-2)


def unfolded(values):
    return jnp.concatenate([values[..., :8, :], values[..., 8:, :]], axis=-1)


def packed(values, ref):
    return values if ref.dtype == F32 else folded(values).astype(ref.dtype)


def lane_fold(values):
    total = values[:, :HEAD]
    for start in range(HEAD, values.shape[1], HEAD):
        total = total + values[:, start : start + HEAD]
    return total


def widen(column, width):
    return jnp.concatenate([column] * (width // HEAD), axis=1)


def kernel(axes, dims, *refs):
    n_grp, n_tx, n_ty = axes
    (
        hid_e, gain_e, wq_e, wk_e, wv_e, wo_e, fin_e, head_e, kc_e, vc_e,
        hid_a, gain_a, wq_a, wk_a, wv_a, wo_a, fin_a, head_a, kc_a, vc_a,
        h_lengths, h_tokens,
        out_ref, score_ref,
        lengths, tokens, v_gain_e, v_fin_e, v_gain_a, v_fin_a,
        v_hid_e, v_wq_e, v_wk_e, v_wv_e, v_wo_e, v_head_e, v_kc_e, v_vc_e,
        v_hid_a, v_wq_a, v_wk_a, v_wv_a, v_wo_a, v_head_a, v_kc_a, v_vc_a,
        x_e, x_a, sq_send, sq_recv,
        p_send_e, p_recv_e, p_send_a, p_recv_a,
        g_e, g_a,
        o_send_e, o_recv_e, o_send_a, o_recv_a,
        s_send_e, s_recv_e, s_send_a, s_recv_a,
        f_e, f_a,
        l_send, l_recv, t_send, t_recv,
        local_sem, ty_send, ty_recv, tx_send, tx_recv, fw_send, fw_recv, l_ssem, l_rsem, t_ssem, t_rsem,
    ) = refs
    grp, tx, ty = lax.axis_index("grp"), lax.axis_index("tx"), lax.axis_index("ty")
    half_rows = v_hid_e.shape[1]
    width_e, width_a = v_hid_e.shape[2], v_hid_a.shape[2]
    heads_e, heads_a = v_wq_e.shape[1] // HEAD, v_wq_a.shape[1] // HEAD
    vocab = head_e.shape[0]

    first = pl.multiple_of(grp * half_rows, half_rows)
    pairs = [
        (hid_e.at[:, pl.ds(first, half_rows)], v_hid_e),
        (hid_a.at[:, pl.ds(first, half_rows)], v_hid_a),
        (h_lengths, lengths), (gain_e, v_gain_e), (gain_a, v_gain_a),
        (fin_e, v_fin_e), (fin_a, v_fin_a), (h_tokens, tokens),
        (wq_a, v_wq_a), (wk_a, v_wk_a), (wv_a, v_wv_a),
        (wq_e, v_wq_e), (wk_e, v_wk_e), (wv_e, v_wv_e),
        (kc_a, v_kc_a), (vc_a, v_vc_a), (kc_e, v_kc_e), (vc_e, v_vc_e),
        (wo_a, v_wo_a), (wo_e, v_wo_e),
        (head_a, v_head_a.at[pl.ds(0, vocab)]), (head_e, v_head_e.at[pl.ds(0, vocab)]),
    ]
    loads = [
        pltpu.make_async_copy(source, target, local_sem.at[number])
        for number, (source, target) in enumerate(pairs)
    ]
    for load in loads[:8]:
        load.start()
    (l_hid_e, l_hid_a, l_lengths, l_gain_e, l_gain_a, l_fin_e, l_fin_a, l_tokens, l_wq_a, l_wk_a, l_wv_a, l_wq_e, l_wk_e, l_wv_e,
     l_kc_a, l_vc_a, l_kc_e, l_vc_e, l_wo_a, l_wo_e, l_head_a, l_head_e) = loads

    def ty_peer(step):
        return lax.rem(ty // 4 + step // 4, n_ty // 4) * 4 + lax.rem(ty + step, 4)

    def tx_peer(step):
        return lax.rem(tx // 4 + step // 4, n_tx // 4) * 4 + lax.rem(tx + step, 4)

    flat = grp * n_tx + tx
    n_flat = n_grp * n_tx

    def flat_peer(step):
        return {"grp": lax.rem(grp + step // n_tx, n_grp), "tx": tx_peer(lax.rem(step, n_tx))}

    def to_ty(step):
        return {"ty": ty_peer(step)}

    def to_tx(step):
        return {"tx": tx_peer(step)}

    def near(step):
        return {"tx": lax.rem(tx // 4 + step // 4, n_tx // 4) * 4 + lax.rem(tx, 4), "ty": ty_peer(step)}

    barrier = pltpu.get_barrier_semaphore()

    def greet(device):
        pl.semaphore_signal(barrier, inc=1, device_id=device, device_id_type=MESH)

    @pl.loop(1, n_ty)
    def _(step):
        greet(to_ty(n_ty - step))

    @pl.loop(4, n_ty)
    def _(step):
        greet(near(step))

    @pl.loop(1, n_flat)
    def _(step):
        greet(flat_peer(n_flat - step))

    for load in loads[8:14]:
        load.start()

    started = []

    class Exchange:
        def __init__(self, n, source, target, send_sem, recv_sem, device, bulk, begin=True, each=False, low=1):
            self.n, self.low = n, low
            self.make = lambda step: pltpu.make_async_remote_copy(
                src_ref=source(step), dst_ref=target(step), send_sem=send_sem,
                recv_sem=recv_sem.at[step] if each else recv_sem, device_id=device(step), device_id_type=MESH,
            )
            self.all = lambda: pltpu.make_async_remote_copy(
                src_ref=bulk, dst_ref=bulk, send_sem=send_sem, recv_sem=recv_sem.at[0] if each else recv_sem,
                device_id=device(low), device_id_type=MESH,
            )
            started.append(self)
            if begin:
                self.begin()

        def begin(self):
            @pl.loop(1, self.n)
            def _(step):
                self.make(self.n - step).start()

        def arrive(self):
            self.all().wait_recv()

        def finish(self):
            self.all().wait_send()

    def drain(keep):
        while len(started) > keep:
            started.pop(0).finish()

    def add_up(exchange, total, recv):
        exchange.arrive()
        for step in range(1, exchange.n):
            total = total + recv[step].astype(F32)
        return total

    n_rows = 2 * half_rows
    block = half_rows // n_ty
    order = one_hot(
        n_rows, lambda o: (o // block) % 2 * half_rows + o // (2 * block) * block + o % block
    )
    l_hid_e.wait()
    wide_e = mm(order, v_hid_e[...].reshape(n_rows, width_e))
    x_e[...] = wide_e.reshape(n_ty, 8, width_e)
    l_hid_a.wait()
    wide_a = mm(order, v_hid_a[...].reshape(n_rows, width_a))
    x_a[...] = wide_a.reshape(n_ty, 8, width_a)
    partial = jnp.concatenate([lane_fold(wide_e * wide_e), lane_fold(wide_a * wide_a)], axis=0)
    own = jnp.broadcast_to(jnp.sum(partial.T, axis=0, keepdims=True), (8, HEAD))
    sq_send[...] = own

    pl.semaphore_wait(barrier, n_ty - 1 + n_ty - 4 + n_flat - 1)

    squares = Exchange(n_ty, lambda d: sq_send, lambda d: sq_recv.at[d], ty_send.at[0], ty_recv.at[0], near,
                       sq_recv.at[pl.ds(1, n_ty - 1)])
    for load in loads[14:18]:
        load.start()

    row8, lane8 = iota((8, HEAD), 0), iota((8, HEAD), 1)
    position = jnp.zeros((8, HEAD), jnp.int32)
    l_lengths.wait()
    for i in range(block):
        position = jnp.where(row8 % block == i, lengths[i], position)
    position = (position + row8 // block).astype(F32)
    exponent = (lane8 % (HEAD // 2)).astype(F32) * (2.0 / HEAD)
    angle = position * jnp.exp(exponent * (-math.log(BASE)))
    cosine = jnp.cos(angle)
    sine = jnp.where(lane8 < HEAD // 2, -1.0, 1.0) * jnp.sin(angle)

    def rotated(values):
        turned = jnp.concatenate([values[:, HEAD // 2 :], values[:, : HEAD // 2]], axis=1)
        return values * cosine + turned * sine

    total = add_up(squares, own, sq_recv)
    square = jnp.broadcast_to(total[0:1], (HEAD, HEAD)).T
    root_e = lax.rsqrt(square[:n_rows] / (width_e * n_ty) + EPS)
    root_a = lax.rsqrt(square[n_rows:] / (width_a * n_ty) + EPS)

    def project(x, root, g_load, gain, weights, send, recv, kind):
        width = x.shape[2]
        g_load.wait()
        values = x[...].reshape(n_rows, width)
        normed = (values * widen(root, width) * gain[...].astype(F32).reshape(1, width)).astype(BF16)
        parts = []
        for load, weight in weights:
            load.wait()
            columns = weight.shape[1]
            for at in range(0, columns, CHUNK):
                parts.append(mm(normed, weight[:, at : at + min(CHUNK, columns - at)]))
        send[...] = packed(jnp.concatenate(parts, axis=1).reshape(n_ty, 8, -1), send)
        return Exchange(n_ty, lambda d: send.at[ty_peer(d)], lambda d: recv.at[d], ty_send.at[kind], ty_recv.at[kind], to_ty,
                        recv.at[pl.ds(1, n_ty - 1)])

    sent_pa = project(x_a, root_a, l_gain_a, v_gain_a, ((l_wq_a, v_wq_a), (l_wk_a, v_wk_a), (l_wv_a, v_wv_a)), p_send_a, p_recv_a, 2)
    sent_pe = project(x_e, root_e, l_gain_e, v_gain_e, ((l_wq_e, v_wq_e), (l_wk_e, v_wk_e), (l_wv_e, v_wv_e)), p_send_e, p_recv_e, 1)

    for load in loads[18:]:
        load.start()

    def summed(exchange, send, recv, me):
        total = add_up(exchange, send[me].astype(F32), recv)
        return total if send.dtype == F32 else unfolded(total)

    def padded(rows, size):
        if rows.shape[0] == size:
            return rows
        return jnp.concatenate([rows, jnp.zeros((size - rows.shape[0], rows.shape[1]), F32)], axis=0)

    def attend(acc, heads, key_heads, k_load, keys, v_load, values):
        group = heads // key_heads
        n_query = heads * 8
        per_row = 2 * heads
        cache = keys.shape[1]
        wide = key_heads * HEAD
        query = jnp.concatenate([rotated(acc[:, h * HEAD : (h + 1) * HEAD]) for h in range(heads)], axis=0)
        at = heads * HEAD
        fresh_k = jnp.concatenate(
            [rotated(acc[:, at + h * HEAD : at + (h + 1) * HEAD]) for h in range(key_heads)], axis=0
        )
        at += wide
        fresh_v = jnp.concatenate(
            [acc[:, at + h * HEAD : at + (h + 1) * HEAD] for h in range(key_heads)], axis=0
        )
        fresh_k = padded(fresh_k, HEAD).astype(BF16)
        fresh_v = padded(fresh_v, HEAD).astype(BF16)
        forth = one_hot(n_query, lambda o: o % heads * 8 + o // heads % 2 * block + o // per_row)
        back = one_hot(n_query, lambda o: o % block * per_row + o // block % 2 * heads + o // 8)
        query = mm(forth, query.astype(BF16))
        owner = iota((n_query, HEAD), 0)
        lane = iota((n_query, HEAD), 1)
        fresh = mm_t(query.astype(BF16), fresh_k) * SCALE
        seen = (
            (lane < key_heads * 8)
            & (lane // 8 == owner % heads // group)
            & (lane % block == owner // per_row)
            & (lane // block % 2 <= owner // heads % 2)
        )
        fresh = jnp.where(seen, fresh, -jnp.inf)
        if key_heads > 1:
            spread = widen(query, wide)
            keep = iota((n_query, wide), 1) // HEAD == iota((n_query, wide), 0) % heads // group
            query = jnp.where(keep, spread, 0.0)
        k_load.wait()
        cached = []
        for i in range(block):
            part = query[i * per_row : (i + 1) * per_row].astype(BF16)
            score = mm_t(part, keys[i]) * SCALE
            cached.append(jnp.where(iota((per_row, cache), 1) < lengths[i], score, -jnp.inf))
        cached = jnp.concatenate(cached, axis=0)
        peak = jnp.maximum(jnp.max(cached, axis=1, keepdims=True), jnp.max(fresh, axis=1, keepdims=True))
        cached = jnp.exp(cached - peak)
        fresh = jnp.exp(fresh - peak)
        total = jnp.sum(cached, axis=1, keepdims=True) + jnp.sum(fresh, axis=1, keepdims=True)
        v_load.wait()
        mixture = jnp.concatenate(
            [mm(cached[i * per_row : (i + 1) * per_row].astype(BF16), values[i]) for i in range(block)], axis=0
        )
        if key_heads > 1:
            picked = jnp.zeros((n_query, HEAD), F32)
            for h in range(key_heads):
                picked = picked + jnp.where(owner % heads // group == h, mixture[:, h * HEAD : (h + 1) * HEAD], 0.0)
            mixture = picked
        mixture = mixture + mm(fresh.astype(BF16), fresh_v)
        ready = mm(back, (mixture / total).astype(BF16))
        return jnp.concatenate([ready[h * 8 : (h + 1) * 8] for h in range(heads)], axis=1)

    def gather(rows, buffer, kind):
        buffer[ty] = folded(rows).astype(BF16)
        return Exchange(n_ty, lambda d: buffer.at[ty], lambda d: buffer.at[ty], ty_send.at[kind], ty_recv.at[kind], to_ty,
                        buffer.at[pl.ds(0, n_ty - 1)])

    acc = summed(sent_pa, p_send_a, p_recv_a, ty)
    sent_ga = gather(attend(acc, heads_a, v_wk_a.shape[1] // HEAD, l_kc_a, v_kc_a, l_vc_a, v_vc_a), g_a, 4)
    acc = summed(sent_pe, p_send_e, p_recv_e, ty)
    sent_ge = gather(attend(acc, heads_e, v_wk_e.shape[1] // HEAD, l_kc_e, v_kc_e, l_vc_e, v_vc_e), g_e, 3)
    drain(2)

    def output(exchange, buffer, load, weight, send, recv, kind):
        exchange.arrive()
        rows = unfolded(buffer[...].astype(F32)).reshape(n_rows, weight.shape[0]).astype(BF16)
        load.wait()
        columns = weight.shape[1]
        parts = [mm(rows, weight[:, at : at + CHUNK]) for at in range(0, columns, CHUNK)]
        send[...] = packed(jnp.concatenate(parts, axis=1).reshape(n_tx, 8, columns), send)
        return Exchange(n_tx, lambda d: send.at[tx_peer(d)], lambda d: recv.at[d], tx_send.at[kind], tx_recv.at[kind, 0], to_tx,
                        recv.at[pl.ds(1, n_tx - 1)])

    sent_oa = output(sent_ga, g_a, l_wo_a, v_wo_a, o_send_a, o_recv_a, 1)
    sent_oe = output(sent_ge, g_e, l_wo_e, v_wo_e, o_send_e, o_recv_e, 0)
    drain(2)

    def residual(exchange, x, send, recv, s_send, s_recv, kind):
        values = x[tx] + summed(exchange, send, recv, tx)
        part = lane_fold(values * values)
        s_send[...] = part
        return values, part, Exchange(
            n_ty, lambda d: s_send, lambda d: s_recv.at[d], ty_send.at[kind], ty_recv.at[kind], to_ty,
            s_recv.at[pl.ds(1, n_ty - 1)],
        )

    res_a, part_a, sent_sa = residual(sent_oa, x_a, o_send_a, o_recv_a, s_send_a, s_recv_a, 6)
    res_e, part_e, sent_se = residual(sent_oe, x_e, o_send_e, o_recv_e, s_send_e, s_recv_e, 5)
    drain(2)

    def final(values, part, exchange, s_recv, g_load, gain, buffer, kind):
        width = values.shape[1]
        g_load.wait()
        part = add_up(exchange, part, s_recv)
        mean = jnp.sum(part, axis=1, keepdims=True) / (width * n_ty)
        rows = values * lax.rsqrt(mean + EPS) * gain[...].astype(F32).reshape(1, width)
        buffer[flat] = folded(rows).astype(BF16)
        across = Exchange(
            n_tx, lambda d: buffer.at[flat], lambda d: buffer.at[flat], tx_send.at[kind], tx_recv.at[kind], to_tx,
            buffer.at[pl.ds(0, n_tx - 1)], each=True,
        )

        def from_tx(step):
            return grp * n_tx + lax.rem(tx // 4 + n_tx // 4 - step // 4, n_tx // 4) * 4 + lax.rem(tx + 4 - lax.rem(step, 4), 4)

        forward = Exchange(
            n_tx, lambda d: buffer.at[from_tx(d)], lambda d: buffer.at[from_tx(d)], fw_send.at[kind - 2],
            fw_recv.at[kind - 2], lambda d: {"grp": 1 - grp}, buffer.at[pl.ds((1 - grp) * n_tx, n_tx)], begin=False, low=0,
        )
        forward.make(0).start()
        return across, forward

    def pass_on(pair):
        across, forward = pair

        @pl.loop(1, n_tx)
        def _(step):
            across.make(step).wait_recv()
            forward.make(step).start()

    def passed_on(pair):
        pair[1].arrive()

    pair_a = final(res_a, part_a, sent_sa, s_recv_a, l_fin_a, v_fin_a, f_a, 3)
    pair_e = final(res_e, part_e, sent_se, s_recv_e, l_fin_e, v_fin_e, f_e, 2)

    padding = v_head_e.shape[0] - vocab
    l_head_a.wait()
    v_head_a[pl.ds(vocab, padding), :] = jnp.zeros((padding, width_a), BF16)
    l_head_e.wait()
    v_head_e[pl.ds(vocab, padding), :] = jnp.zeros((padding, width_e), BF16)

    n_slab = v_head_e.shape[0] // SLAB

    logit_exchanges = [
        Exchange(
            n_ty, lambda d, slab=slab: l_send.at[slab, ty_peer(d)], lambda d, slab=slab: l_recv.at[slab, d], l_ssem.at[slab],
            l_rsem.at[slab], to_ty, l_recv.at[slab, pl.ds(1, n_ty - 1)], begin=False,
        )
        for slab in range(2 * n_slab)
    ]

    own_coarse = ty // 4 == grp
    first_from, first_to = jnp.where(own_coarse, 1, 4), jnp.where(own_coarse, 4, n_ty)
    second_from, second_to = jnp.where(own_coarse, 4, 1), jnp.where(own_coarse, n_ty, 4)

    def logits(buffer, half, head, base, low, high):
        rows = unfolded(buffer[pl.ds(half * n_tx, n_tx)].astype(F32)).reshape(n_rows, head.shape[1]).astype(BF16)
        for slab in range(n_slab):
            for at in range(0, SLAB, CHUNK):
                part = mm_t(rows, head[slab * SLAB + at : slab * SLAB + at + CHUNK, :])
                part = part.reshape(n_ty // n_grp, 16, CHUNK).astype(BF16)
                l_send[base + slab, pl.ds(half * (n_ty // n_grp), n_ty // n_grp), :, at : at + CHUNK] = part
            exchange = logit_exchanges[base + slab]

            @pl.loop(low, high)
            def _(step):
                exchange.make(step).start()

    pass_on(pair_a)
    logits(f_a, grp, v_head_a, n_slab, first_from, first_to)
    passed_on(pair_a)
    logits(f_a, 1 - grp, v_head_a, n_slab, second_from, second_to)
    pass_on(pair_e)
    logits(f_e, grp, v_head_e, 0, first_from, first_to)
    passed_on(pair_e)
    logits(f_e, 1 - grp, v_head_e, 0, second_from, second_to)

    def slab_sum(slab):
        return add_up(logit_exchanges[slab], l_send[slab, ty].astype(F32), l_recv.at[slab])

    lane_c = iota((16, SLAB), 1)

    def peak_and_total(parts):
        masked = [jnp.where(lane_c + c * SLAB < vocab, part, -jnp.inf) for c, part in enumerate(parts)]
        peak = masked[0]
        for part in masked[1:]:
            peak = jnp.maximum(peak, part)
        peak = jnp.max(peak, axis=1, keepdims=True)
        total = jnp.exp(masked[0] - peak)
        for part in masked[1:]:
            total = total + jnp.exp(part - peak)
        return peak, jnp.sum(total, axis=1, keepdims=True)

    l_tokens.wait()
    row16 = iota((16, HEAD), 0)
    token = jnp.zeros((16, HEAD), jnp.int32)
    for s in range(2):
        for r in range(8):
            token = jnp.where(row16 == r // block * 8 + s * block + r % block, tokens[s, r], token)
    token = widen(token - flat * vocab, SLAB)

    drain(2 * n_slab)
    amateur = [slab_sum(n_slab + c) for c in range(n_slab)]
    peak_a, total_a = peak_and_total(amateur)
    expert = [slab_sum(c) for c in range(n_slab)]
    peak_e, total_e = peak_and_total(expert)
    chosen = jnp.zeros((16, SLAB), F32)
    mixed = []
    for c in range(n_slab):
        mixed.append(expert[c] - AMATEUR * amateur[c])
        column = lane_c + c * SLAB
        chosen = chosen + jnp.where((column == token) & (column < vocab), mixed[c], 0.0)
    chosen = jnp.sum(chosen, axis=1, keepdims=True)

    lane16 = iota((16, HEAD), 1) % 64
    tile = jnp.where(lane16 == 0, peak_e, jnp.where(lane16 == 1, total_e, 0.0))
    tile = jnp.where(lane16 == 2, peak_a, jnp.where(lane16 == 3, total_a, tile))
    tile = jnp.where(lane16 == 4, chosen, tile)
    tile = jnp.where(lane8 < 64, tile[:8], tile[8:])
    t_send[...] = tile
    stats = Exchange(n_flat, lambda d: t_send, lambda d: t_recv.at[d], t_ssem.at[0], t_rsem.at[0], flat_peer,
             t_recv.at[pl.ds(1, n_flat - 1)])
    drain(1)
    stats.arrive()
    tiles = [tile] + [t_recv[step] for step in range(1, n_flat)]
    highest = functools.reduce(jnp.maximum, tiles)
    picked = functools.reduce(jnp.add, tiles)

    def shifted(values):
        return jnp.concatenate([values[:, 1:], values[:, :1]], axis=1)

    summed_up = functools.reduce(jnp.add, [jnp.exp(t - highest) * shifted(t) for t in tiles])
    log_total = highest + jnp.log(summed_up)

    def column(values, lane):
        return jnp.concatenate([values[:, lane : lane + 1], values[:, lane + 64 : lane + 65]], axis=0)

    offset = column(log_total, 0) - AMATEUR * column(log_total, 2)
    for c in range(n_slab):
        size = min(SLAB, vocab - c * SLAB)
        contrast = mixed[c] - offset
        for s in range(2):
            low = s * block
            out_ref[s, :, c * SLAB : c * SLAB + size] = jnp.concatenate(
                [contrast[low : low + block], contrast[8 + low : 8 + low + block]], axis=0
            )[:, :size]
    value = jnp.broadcast_to(column(picked, 4) - offset, (16, HEAD))
    lane_r = iota((16, HEAD), 1)
    for s in range(2):
        mine = row16 == lane_r // block * 8 + s * block + lane_r % block
        line = jnp.sum(jnp.where(mine & (lane_r < 8), value, 0.0), axis=0, keepdims=True)
        score_ref[s : s + 1, :] = line[:, :8]

    drain(0)


def on_device(axes, *args):
    (
        hid_e, gain_e, wq_e, wk_e, wv_e, wo_e, fin_e, head_e, kc_e, vc_e,
        hid_a, gain_a, wq_a, wk_a, wv_a, wo_a, fin_a, head_a, kc_a, vc_a,
        lengths, tokens,
    ) = args
    n_grp, n_tx, n_ty = axes
    n_flat = n_grp * n_tx
    half = hid_e.shape[1] // n_grp
    vocab = head_e.shape[0]
    padded = -(-vocab // SLAB) * SLAB
    n_slab = padded // SLAB
    n_rows = 2 * half
    width_e, width_a = hid_e.shape[2], hid_a.shape[2]
    cols_e = wq_e.shape[1] + wk_e.shape[1] + wv_e.shape[1]
    cols_a = wq_a.shape[1] + wk_a.shape[1] + wv_a.shape[1]
    inner_e, inner_a = wo_e.shape[0], wo_a.shape[0]

    def like(array):
        return pltpu.VMEM(array.shape, array.dtype)

    scratch = [
        pltpu.SMEM(lengths.shape, jnp.int32), pltpu.SMEM(tokens.shape, jnp.int32),
        like(gain_e), like(fin_e), like(gain_a), like(fin_a),
    ]
    for hid, wq, wk, wv, wo, head, kc, vc in (
        (hid_e, wq_e, wk_e, wv_e, wo_e, head_e, kc_e, vc_e),
        (hid_a, wq_a, wk_a, wv_a, wo_a, head_a, kc_a, vc_a),
    ):
        scratch += [
            pltpu.VMEM((2, half, hid.shape[2]), BF16), like(wq), like(wk), like(wv), like(wo),
            pltpu.VMEM((padded, head.shape[1]), BF16), like(kc), like(vc),
        ]
    scratch += [
        pltpu.VMEM((n_ty, 8, width_e), F32), pltpu.VMEM((n_ty, 8, width_a), F32),
        pltpu.VMEM((8, HEAD), F32), pltpu.VMEM((n_ty, 8, HEAD), F32),
        pltpu.VMEM((n_ty, 8, cols_e), F32), pltpu.VMEM((n_ty, 8, cols_e), F32),
        pltpu.VMEM((n_ty, 16, cols_a // 2), BF16), pltpu.VMEM((n_ty, 16, cols_a // 2), BF16),
        pltpu.VMEM((n_ty, 16, inner_e // 2), BF16), pltpu.VMEM((n_ty, 16, inner_a // 2), BF16),
        pltpu.VMEM((n_tx, 16, width_e // 2), BF16), pltpu.VMEM((n_tx, 16, width_e // 2), BF16),
        pltpu.VMEM((n_tx, 16, width_a // 2), BF16), pltpu.VMEM((n_tx, 16, width_a // 2), BF16),
        pltpu.VMEM((8, HEAD), F32), pltpu.VMEM((n_ty, 8, HEAD), F32),
        pltpu.VMEM((8, HEAD), F32), pltpu.VMEM((n_ty, 8, HEAD), F32),
        pltpu.VMEM((n_flat, 16, width_e // 2), BF16), pltpu.VMEM((n_flat, 16, width_a // 2), BF16),
        pltpu.VMEM((2 * n_slab, n_ty, 16, SLAB), BF16), pltpu.VMEM((2 * n_slab, n_ty, 16, SLAB), BF16),
        pltpu.VMEM((8, HEAD), F32), pltpu.VMEM((n_flat, 8, HEAD), F32),
        pltpu.SemaphoreType.DMA((22,)),
        pltpu.SemaphoreType.DMA((7,)), pltpu.SemaphoreType.DMA((7,)),
        pltpu.SemaphoreType.DMA((4,)), pltpu.SemaphoreType.DMA((4, n_tx)),
        pltpu.SemaphoreType.DMA((2,)), pltpu.SemaphoreType.DMA((2,)),
        pltpu.SemaphoreType.DMA((2 * n_slab,)), pltpu.SemaphoreType.DMA((2 * n_slab,)),
        pltpu.SemaphoreType.DMA((1,)), pltpu.SemaphoreType.DMA((1,)),
    ]
    hbm = pl.BlockSpec(memory_space=pl.ANY)
    vmem = pl.BlockSpec(memory_space=pltpu.VMEM)
    macs = n_rows * (width_e * (cols_e + inner_e) + width_a * (cols_a + inner_a)) + 2 * n_rows * vocab * (width_e + width_a)
    read = sum(array.size * array.dtype.itemsize for array in args)
    return pl.pallas_call(
        functools.partial(kernel, axes, None),
        out_shape=(
            jax.ShapeDtypeStruct((2, hid_e.shape[1] // n_ty, vocab), F32),
            jax.ShapeDtypeStruct((2, hid_e.shape[1] // n_ty), F32),
        ),
        in_specs=[hbm] * len(args),
        out_specs=(vmem, vmem),
        scratch_shapes=scratch,
        compiler_params=pltpu.CompilerParams(
            collective_id=0, has_side_effects=True, vmem_limit_bytes=56 * 1024 * 1024
        ),
        cost_estimate=pl.CostEstimate(flops=2 * macs, bytes_accessed=read, transcendentals=0),
        name="contrast",
    )(*args)


def solution(mesh):
    model = (
        P(None, None, "ty"), P("ty"), P("ty", "tx"), P("ty", "tx"), P("ty", "tx"), P("tx", "ty"), P("ty"),
        P(("grp", "tx"), "ty"), P(("grp", "ty"), None, "tx"), P(("grp", "ty"), None, "tx"),
    )
    axes = tuple(mesh.shape[name] for name in ("grp", "tx", "ty"))
    return jax.shard_map(
        functools.partial(on_device, axes),
        mesh=mesh,
        in_specs=model + model + (P(("grp", "ty")), P(None, "ty")),
        out_specs=(P(None, "ty", ("grp", "tx")), P(None, "ty")),
        check_vma=False,
    )
```

profile of v0, /device:TPU:1, one launch (start us, length us, event | category | flops | bytes accessed | tf_op | source)
XLA Modules:
  0.0 64.3 jit_solution(11765847947385854611)
XLA Ops:
  0.6 60.8 %contrast.1 = (f32[2,8,2000]{2,1,0:T(8,128)}, f32[2,8]{1,0:T(2,128)}) custom-call(bf16[2,64,1024]{2,1,0:T(8,128)(2,1)} %refs_0_.1, bf16[1024]{0:T(1024)(128)(2,1)} %refs_1_.1, bf16[1024,1024]{1,0:T(8,128)(2,1)} %refs_2_.1, bf16[1024,128]{1,0:T(8,128)(2,1)} %refs_3_.1, bf16[1024,128]{1,0:T(8,128)(2,1)} %refs_4_.1, bf16[1024,1024]{1,0:T(8,128)(2,1)} %refs_5_.1, ...), custom_call_target="tpu_custom_call" | custom-call | flops 1222639616 | bytes 23844944 | tf_op jit(solution)/shard_map/contrast/pallas_call | solution.py:571
  61.5 1.6 %copy.26 = f32[2,8,2000]{2,1,0:T(8,128)} copy(f32[2,8,2000]{2,1,0:T(8,128)} %get-tuple-element.4) | data formatting | bytes 256000
  63.0 1.2 %copy.27 = f32[2,8]{1,0:T(2,128)} copy(f32[2,8]{1,0:T(2,128)} %get-tuple-element.5) | data formatting | bytes 128
where the time goes:
time: 64.4 us; the launch traced here: 64.3 us
  Pallas kernels  60.8 us (94%)
  local copies, waits for them, and re-layouts  2.8 us (4%)
  between operations  0.65 us (1%)
    pallas_call x1, Pallas kernels, on_device(): pl.pallas_call(functools.partial(kernel, axes, None), out_shape=(jax.Shap...  60.8 us
    unnamed x2, local copies, waits for them, and re-layouts  2.8 us

commit v1 on v0

--- a/solution.py
+++ b/solution.py
@@ -107,43 +107,40 @@
     (l_hid_e, l_hid_a, l_lengths, l_gain_e, l_gain_a, l_fin_e, l_fin_a, l_tokens, l_wq_a, l_wk_a, l_wv_a, l_wq_e, l_wk_e, l_wv_e,
      l_kc_a, l_vc_a, l_kc_e, l_vc_e, l_wo_a, l_wo_e, l_head_a, l_head_e) = loads
 
-    def ty_peer(step):
-        return lax.rem(ty // 4 + step // 4, n_ty // 4) * 4 + lax.rem(ty + step, 4)
-
-    def tx_peer(step):
-        return lax.rem(tx // 4 + step // 4, n_tx // 4) * 4 + lax.rem(tx + step, 4)
-
+    coarse, ring = ty // 4, lax.rem(ty, 4)
+    tx_coarse, tx_ring = tx // 4, lax.rem(tx, 4)
+    rings = [lax.rem(ring + step, 4) for step in range(4)]
+    ty_peers = [lax.rem(coarse + step // 4, n_ty // 4) * 4 + rings[step % 4] for step in range(n_ty)]
+    tx_rings = [lax.rem(tx_ring + step, 4) for step in range(4)]
+    tx_sides = [lax.rem(tx_coarse + step, n_tx // 4) * 4 for step in range(n_tx // 4)]
+    tx_peers = [tx_sides[step // 4] + tx_rings[step % 4] for step in range(n_tx)]
+    tx_sources = [tx_sides[step // 4] + tx_rings[-step % 4] for step in range(n_tx)]
     flat = grp * n_tx + tx
     n_flat = n_grp * n_tx
 
+    def to_ty(step):
+        return {"ty": ty_peers[step]}
+
+    def to_tx(step):
+        return {"tx": tx_peers[step]}
+
     def flat_peer(step):
-        return {"grp": lax.rem(grp + step // n_tx, n_grp), "tx": tx_peer(lax.rem(step, n_tx))}
-
-    def to_ty(step):
-        return {"ty": ty_peer(step)}
-
-    def to_tx(step):
-        return {"tx": tx_peer(step)}
+        return {"grp": lax.rem(grp + step // n_tx, n_grp), "tx": tx_peers[step % n_tx]}
 
     def near(step):
-        return {"tx": lax.rem(tx // 4 + step // 4, n_tx // 4) * 4 + lax.rem(tx, 4), "ty": ty_peer(step)}
+        return {"tx": tx_sides[step // 4] + tx_ring, "ty": ty_peers[step]}
 
     barrier = pltpu.get_barrier_semaphore()
 
     def greet(device):
         pl.semaphore_signal(barrier, inc=1, device_id=device, device_id_type=MESH)
 
-    @pl.loop(1, n_ty)
-    def _(step):
-        greet(to_ty(n_ty - step))
-
-    @pl.loop(4, n_ty)
-    def _(step):
+    for step in range(n_ty - 1, 0, -1):
         greet(near(step))
-
-    @pl.loop(1, n_flat)
-    def _(step):
-        greet(flat_peer(n_flat - step))
+    for step in range(4, n_ty):
+        greet(to_ty(step))
+    for step in range(n_flat - 1, 0, -1):
+        greet(flat_peer(step))
 
     for load in loads[8:14]:
         load.start()
@@ -166,9 +163,8 @@
                 self.begin()
 
         def begin(self):
-            @pl.loop(1, self.n)
-            def _(step):
-                self.make(self.n - step).start()
+            for step in range(self.n - 1, 0, -1):
+                self.make(step).start()
 
         def arrive(self):
             self.all().wait_recv()
@@ -240,7 +236,7 @@
             for at in range(0, columns, CHUNK):
                 parts.append(mm(normed, weight[:, at : at + min(CHUNK, columns - at)]))
         send[...] = packed(jnp.concatenate(parts, axis=1).reshape(n_ty, 8, -1), send)
-        return Exchange(n_ty, lambda d: send.at[ty_peer(d)], lambda d: recv.at[d], ty_send.at[kind], ty_recv.at[kind], to_ty,
+        return Exchange(n_ty, lambda d: send.at[ty_peers[d]], lambda d: recv.at[d], ty_send.at[kind], ty_recv.at[kind], to_ty,
                         recv.at[pl.ds(1, n_ty - 1)])
 
     sent_pa = project(x_a, root_a, l_gain_a, v_gain_a, ((l_wq_a, v_wq_a), (l_wk_a, v_wk_a), (l_wv_a, v_wv_a)), p_send_a, p_recv_a, 2)
@@ -334,7 +330,7 @@
         columns = weight.shape[1]
         parts = [mm(rows, weight[:, at : at + CHUNK]) for at in range(0, columns, CHUNK)]
         send[...] = packed(jnp.concatenate(parts, axis=1).reshape(n_tx, 8, columns), send)
-        return Exchange(n_tx, lambda d: send.at[tx_peer(d)], lambda d: recv.at[d], tx_send.at[kind], tx_recv.at[kind, 0], to_tx,
+        return Exchange(n_tx, lambda d: send.at[tx_peers[d]], lambda d: recv.at[d], tx_send.at[kind], tx_recv.at[kind, 0], to_tx,
                         recv.at[pl.ds(1, n_tx - 1)])
 
     sent_oa = output(sent_ga, g_a, l_wo_a, v_wo_a, o_send_a, o_recv_a, 1)
@@ -367,7 +363,7 @@
         )
 
         def from_tx(step):
-            return grp * n_tx + lax.rem(tx // 4 + n_tx // 4 - step // 4, n_tx // 4) * 4 + lax.rem(tx + 4 - lax.rem(step, 4), 4)
+            return grp * n_tx + tx_sources[step]
 
         forward = Exchange(
             n_tx, lambda d: buffer.at[from_tx(d)], lambda d: buffer.at[from_tx(d)], fw_send.at[kind - 2],
@@ -379,8 +375,7 @@
     def pass_on(pair):
         across, forward = pair
 
-        @pl.loop(1, n_tx)
-        def _(step):
+        for step in (1, 3, 4, 2, 5, 7, 6):
             across.make(step).wait_recv()
             forward.make(step).start()
 
@@ -400,37 +395,42 @@
 
     logit_exchanges = [
         Exchange(
-            n_ty, lambda d, slab=slab: l_send.at[slab, ty_peer(d)], lambda d, slab=slab: l_recv.at[slab, d], l_ssem.at[slab],
-            l_rsem.at[slab], to_ty, l_recv.at[slab, pl.ds(1, n_ty - 1)], begin=False,
+            n_ty, None, None, l_ssem.at[slab], l_rsem.at[slab], to_ty, l_recv.at[slab, pl.ds(1, n_ty - 1)], begin=False,
         )
         for slab in range(2 * n_slab)
     ]
 
-    own_coarse = ty // 4 == grp
-    first_from, first_to = jnp.where(own_coarse, 1, 4), jnp.where(own_coarse, 4, n_ty)
-    second_from, second_to = jnp.where(own_coarse, 4, 1), jnp.where(own_coarse, n_ty, 4)
-
-    def logits(buffer, half, head, base, low, high):
+    def logits(buffer, half, head, base):
         rows = unfolded(buffer[pl.ds(half * n_tx, n_tx)].astype(F32)).reshape(n_rows, head.shape[1]).astype(BF16)
+        side = jnp.where(half == coarse, 0, 4)
+
+        def copy(slab, step):
+            target = half * 4 + rings[step]
+            return pltpu.make_async_remote_copy(
+                src_ref=l_send.at[slab, target], dst_ref=l_recv.at[slab, side + step], send_sem=l_ssem.at[slab],
+                recv_sem=l_rsem.at[slab], device_id={"ty": target}, device_id_type=MESH,
+            )
+
         for slab in range(n_slab):
             for at in range(0, SLAB, CHUNK):
                 part = mm_t(rows, head[slab * SLAB + at : slab * SLAB + at + CHUNK, :])
-                part = part.reshape(n_ty // n_grp, 16, CHUNK).astype(BF16)
-                l_send[base + slab, pl.ds(half * (n_ty // n_grp), n_ty // n_grp), :, at : at + CHUNK] = part
-            exchange = logit_exchanges[base + slab]
-
-            @pl.loop(low, high)
-            def _(step):
-                exchange.make(step).start()
+                part = part.reshape(4, 16, CHUNK).astype(BF16)
+                l_send[base + slab, pl.ds(half * 4, 4), :, at : at + CHUNK] = part
+            for step in (2, 1, 3):
+                copy(base + slab, step).start()
+
+            @pl.when(half != coarse)
+            def _():
+                copy(base + slab, 0).start()
 
     pass_on(pair_a)
-    logits(f_a, grp, v_head_a, n_slab, first_from, first_to)
+    logits(f_a, grp, v_head_a, n_slab)
+    pass_on(pair_e)
     passed_on(pair_a)
-    logits(f_a, 1 - grp, v_head_a, n_slab, second_from, second_to)
-    pass_on(pair_e)
-    logits(f_e, grp, v_head_e, 0, first_from, first_to)
+    logits(f_a, 1 - grp, v_head_a, n_slab)
+    logits(f_e, grp, v_head_e, 0)
     passed_on(pair_e)
-    logits(f_e, 1 - grp, v_head_e, 0, second_from, second_to)
+    logits(f_e, 1 - grp, v_head_e, 0)
 
     def slab_sum(slab):
         return add_up(logit_exchanges[slab], l_send[slab, ty].astype(F32), l_recv.at[slab])
@@ -571,8 +571,8 @@
     return pl.pallas_call(
         functools.partial(kernel, axes, None),
         out_shape=(
-            jax.ShapeDtypeStruct((2, hid_e.shape[1] // n_ty, vocab), F32),
-            jax.ShapeDtypeStruct((2, hid_e.shape[1] // n_ty), F32),
+            pltpu.VMEM((2, hid_e.shape[1] // n_ty, vocab), F32),
+            pltpu.VMEM((2, hid_e.shape[1] // n_ty), F32),
         ),
         in_specs=[hbm] * len(args),
         out_specs=(vmem, vmem),

time: 64.4 us -> 62.1 us (0.964)
  local copies, waits for them, and re-layouts: 2.8 us -> 1.22 us
  Pallas kernels: 60.8 us -> 60.1 us
    unnamed x2, local copies, waits for them, and re-layouts: 2.8 us -> 1.22 us
    pallas_call x1, Pallas kernels: 60.8 us -> 60.1 us  [on_device(): pl.pallas_call(functools.partial(kernel, axes, None), out_shape=(pltpu.VM...]
where the time goes in v1:
time: 62.1 us; the launch traced here: 62 us
  Pallas kernels  60.1 us (97%)
  local copies, waits for them, and re-layouts  1.22 us (2%)
  between operations  0.65 us (1%)
    pallas_call x1, Pallas kernels, on_device(): pl.pallas_call(functools.partial(kernel, axes, None), out_shape=(pltpu.VM...  60.1 us

profile of v1, /device:TPU:1, one launch (start us, length us, event | category | flops | bytes accessed | tf_op | source)
XLA Modules:
  0.0 62.0 jit_solution(11153725726865719256)
XLA Ops:
  0.6 60.1 %contrast.1 = (f32[2,8,2000]{2,1,0:T(8,128)S(1)}, f32[2,8]{1,0:T(2,128)S(1)}) custom-call(bf16[2,64,1024]{2,1,0:T(8,128)(2,1)} %refs_0_.1, bf16[1024]{0:T(1024)(128)(2,1)} %refs_1_.1, bf16[1024,1024]{1,0:T(8,128)(2,1)} %refs_2_.1, bf16[1024,128]{1,0:T(8,128)(2,1)} %refs_3_.1, bf16[1024,128]{1,0:T(8,128)(2,1)} %refs_4_.1, bf16[1024,1024]{1,0:T(8,128)(2,1)} %refs_5_.1, ...), custom_call_target="tpu_custom_call" | custom-call | flops 1222639616 | bytes 23844944 | tf_op jit(solution)/shard_map/contrast/pallas_call | solution.py:571
  60.8 0.7 %copy.26 = f32[2,8,2000]{2,1,0:T(8,128)} copy(f32[2,8,2000]{2,1,0:T(8,128)S(1)} %get-tuple-element.2) | data formatting | bytes 256000
  61.4 0.6 copy.27

commit v2 on v1

--- a/solution.py
+++ b/solution.py
@@ -102,7 +102,7 @@
         pltpu.make_async_copy(source, target, local_sem.at[number])
         for number, (source, target) in enumerate(pairs)
     ]
-    for load in loads[:8]:
+    for load in loads[:2]:
         load.start()
     (l_hid_e, l_hid_a, l_lengths, l_gain_e, l_gain_a, l_fin_e, l_fin_a, l_tokens, l_wq_a, l_wk_a, l_wv_a, l_wq_e, l_wk_e, l_wv_e,
      l_kc_a, l_vc_a, l_kc_e, l_vc_e, l_wo_a, l_wo_e, l_head_a, l_head_e) = loads
@@ -142,7 +142,7 @@
     for step in range(n_flat - 1, 0, -1):
         greet(flat_peer(step))
 
-    for load in loads[8:14]:
+    for load in loads[2:14]:
         load.start()
 
     started = []
@@ -257,7 +257,6 @@
     def attend(acc, heads, key_heads, k_load, keys, v_load, values):
         group = heads // key_heads
         n_query = heads * 8
-        per_row = 2 * heads
         cache = keys.shape[1]
         wide = key_heads * HEAD
         query = jnp.concatenate([rotated(acc[:, h * HEAD : (h + 1) * HEAD]) for h in range(heads)], axis=0)
@@ -271,45 +270,47 @@
         )
         fresh_k = padded(fresh_k, HEAD).astype(BF16)
         fresh_v = padded(fresh_v, HEAD).astype(BF16)
-        forth = one_hot(n_query, lambda o: o % heads * 8 + o // heads % 2 * block + o // per_row)
-        back = one_hot(n_query, lambda o: o % block * per_row + o // block % 2 * heads + o // 8)
-        query = mm(forth, query.astype(BF16))
         owner = iota((n_query, HEAD), 0)
         lane = iota((n_query, HEAD), 1)
         fresh = mm_t(query.astype(BF16), fresh_k) * SCALE
         seen = (
             (lane < key_heads * 8)
-            & (lane // 8 == owner % heads // group)
-            & (lane % block == owner // per_row)
-            & (lane // block % 2 <= owner // heads % 2)
+            & (lane // 8 == owner // 8 // group)
+            & (lane % block == owner % block)
+            & (lane // block % 2 <= owner // block % 2)
         )
         fresh = jnp.where(seen, fresh, -jnp.inf)
         if key_heads > 1:
-            spread = widen(query, wide)
-            keep = iota((n_query, wide), 1) // HEAD == iota((n_query, wide), 0) % heads // group
-            query = jnp.where(keep, spread, 0.0)
+            keep = iota((n_query, wide), 1) // HEAD == iota((n_query, wide), 0) // 8 // group
+            query = jnp.where(keep, widen(query, wide), 0.0)
+        query = query.astype(BF16)
+        length = jnp.zeros((n_query, HEAD), jnp.int32)
+        for i in range(block):
+            length = jnp.where(owner % block == i, lengths[i], length)
+
+        def of_own_row(operand, rows, multiply):
+            picked = None
+            for i in range(block):
+                part = multiply(operand, rows[i])
+                own = widen(owner % block == i, part.shape[1])
+                picked = part if i == 0 else jnp.where(own, part, picked)
+            return picked
+
         k_load.wait()
-        cached = []
-        for i in range(block):
-            part = query[i * per_row : (i + 1) * per_row].astype(BF16)
-            score = mm_t(part, keys[i]) * SCALE
-            cached.append(jnp.where(iota((per_row, cache), 1) < lengths[i], score, -jnp.inf))
-        cached = jnp.concatenate(cached, axis=0)
+        cached = of_own_row(query, keys, mm_t) * SCALE
+        cached = jnp.where(iota((n_query, cache), 1) < widen(length, cache), cached, -jnp.inf)
         peak = jnp.maximum(jnp.max(cached, axis=1, keepdims=True), jnp.max(fresh, axis=1, keepdims=True))
         cached = jnp.exp(cached - peak)
         fresh = jnp.exp(fresh - peak)
         total = jnp.sum(cached, axis=1, keepdims=True) + jnp.sum(fresh, axis=1, keepdims=True)
         v_load.wait()
-        mixture = jnp.concatenate(
-            [mm(cached[i * per_row : (i + 1) * per_row].astype(BF16), values[i]) for i in range(block)], axis=0
-        )
+        mixture = of_own_row(cached.astype(BF16), values, mm)
         if key_heads > 1:
             picked = jnp.zeros((n_query, HEAD), F32)
             for h in range(key_heads):
-                picked = picked + jnp.where(owner % heads // group == h, mixture[:, h * HEAD : (h + 1) * HEAD], 0.0)
+                picked = picked + jnp.where(owner // 8 // group == h, mixture[:, h * HEAD : (h + 1) * HEAD], 0.0)
             mixture = picked
-        mixture = mixture + mm(fresh.astype(BF16), fresh_v)
-        ready = mm(back, (mixture / total).astype(BF16))
+        ready = (mixture + mm(fresh.astype(BF16), fresh_v)) / total
         return jnp.concatenate([ready[h * 8 : (h + 1) * 8] for h in range(heads)], axis=1)
 
     def gather(rows, buffer, kind):
@@ -437,16 +438,14 @@
 
     lane_c = iota((16, SLAB), 1)
 
-    def peak_and_total(parts):
-        masked = [jnp.where(lane_c + c * SLAB < vocab, part, -jnp.inf) for c, part in enumerate(parts)]
-        peak = masked[0]
-        for part in masked[1:]:
-            peak = jnp.maximum(peak, part)
-        peak = jnp.max(peak, axis=1, keepdims=True)
-        total = jnp.exp(masked[0] - peak)
-        for part in masked[1:]:
-            total = total + jnp.exp(part - peak)
-        return peak, jnp.sum(total, axis=1, keepdims=True)
+    def peak_and_total(part, c):
+        masked = jnp.where(lane_c + c * SLAB < vocab, part, -jnp.inf)
+        peak = jnp.max(masked, axis=1, keepdims=True)
+        return peak, jnp.sum(jnp.exp(masked - peak), axis=1, keepdims=True)
+
+    def merged(pairs):
+        peak = functools.reduce(jnp.maximum, [peak for peak, _ in pairs])
+        return peak, functools.reduce(jnp.add, [total * jnp.exp(own - peak) for own, total in pairs])
 
     l_tokens.wait()
     row16 = iota((16, HEAD), 0)
@@ -458,15 +457,16 @@
 
     drain(2 * n_slab)
     amateur = [slab_sum(n_slab + c) for c in range(n_slab)]
-    peak_a, total_a = peak_and_total(amateur)
-    expert = [slab_sum(c) for c in range(n_slab)]
-    peak_e, total_e = peak_and_total(expert)
+    peak_a, total_a = merged([peak_and_total(amateur[c], c) for c in range(n_slab)])
     chosen = jnp.zeros((16, SLAB), F32)
-    mixed = []
+    mixed, pairs = [], []
     for c in range(n_slab):
-        mixed.append(expert[c] - AMATEUR * amateur[c])
+        expert = slab_sum(c)
+        pairs.append(peak_and_total(expert, c))
+        mixed.append(expert - AMATEUR * amateur[c])
         column = lane_c + c * SLAB
         chosen = chosen + jnp.where((column == token) & (column < vocab), mixed[c], 0.0)
+    peak_e, total_e = merged(pairs)
     chosen = jnp.sum(chosen, axis=1, keepdims=True)
 
     lane16 = iota((16, HEAD), 1) % 64

time: 62.1 us -> 62.1 us (level)
  no operation moved by 1% of the time
where the time goes in v2:
time: 62.1 us; the launch traced here: 62 us
  Pallas kernels  60.2 us (97%)
  local copies, waits for them, and re-layouts  1.22 us (2%)
  between operations  0.65 us (1%)
    pallas_call x1, Pallas kernels, on_device(): pl.pallas_call(functools.partial(kernel, axes, None), out_shape=(pltpu.VM...  60.2 us

profile of v2, /device:TPU:1, one launch (start us, length us, event | category | flops | bytes accessed | tf_op | source)
XLA Modules:
  0.0 62.0 jit_solution(9543299607624631582)
XLA Ops:
  0.6 60.2 %contrast.1 = (f32[2,8,2000]{2,1,0:T(8,128)S(1)}, f32[2,8]{1,0:T(2,128)S(1)}) custom-call(bf16[2,64,1024]{2,1,0:T(8,128)(2,1)} %refs_0_.1, bf16[1024]{0:T(1024)(128)(2,1)} %refs_1_.1, bf16[1024,1024]{1,0:T(8,128)(2,1)} %refs_2_.1, bf16[1024,128]{1,0:T(8,128)(2,1)} %refs_3_.1, bf16[1024,128]{1,0:T(8,128)(2,1)} %refs_4_.1, bf16[1024,1024]{1,0:T(8,128)(2,1)} %refs_5_.1, ...), custom_call_target="tpu_custom_call" | custom-call | flops 1222639616 | bytes 23844944 | tf_op jit(solution)/shard_map/contrast/pallas_call | solution.py:571
  60.8 0.7 %copy.26 = f32[2,8,2000]{2,1,0:T(8,128)} copy(f32[2,8,2000]{2,1,0:T(8,128)S(1)} %get-tuple-element.2) | data formatting | bytes 256000
  61.5 0.6 copy.27
